TPU v7x, 128 devices: a whole 4x4x4 slice. The times are simulated.
128 devices in a mesh: dp: 8 (over x, core), help: 16 (over y, z).
Axes of the slice: x: 4, y: 4, z: 4, core: 2. Of those that a mesh axis runs over, the one named last changes fastest.
Arguments:
- coeffs: bfloat16 [8, 1024, 9, 256], P('dp', 'help'), may hold values from -6 to 6
- cotangent: bfloat16 [8, 1024, 9, 256], P('dp', 'help'), may hold values from -6 to 6
- w_zero: bfloat16 [768, 768], replicated, may hold values from -0.21875 to 0.21875
- w_one: bfloat16 [2, 512, 512], replicated, may hold values from -0.25 to 0.25
- w_two: bfloat16 [2, 256, 256], replicated, may hold values from -0.375 to 0.375
- source: int32 [8, 16384], P('dp', 'help'), may hold values from 0 to 191, as said below
- target: int32 [8, 16384], P('dp', 'help'), may hold values from 0 to 63
- rotation: bfloat16 [8, 35, 16384], P('dp', None, 'help'), may hold values from -3 to 3
- gate: bfloat16 [8, 16384], P('dp', 'help'), may hold values from 0.099609375 to 0.5
- tile_live: int32 [8, 256], P('dp', 'help'), may hold values from 0 to 1, as said below
Outputs:
- updated: bfloat16 [8, 1024, 9, 256], P('dp', 'help')
- grad_coeffs: bfloat16 [8, 1024, 9, 256], P('dp', 'help')
- grad_w_zero: float32 [768, 768], replicated
- grad_w_one: float32 [2, 512, 512], replicated
- grad_w_two: float32 [2, 256, 256], replicated
Inputs may be any that keep to these rules, and one draw needn't show every extreme that they name: `source`: indices 0 to 63 name the block of the device before along help, then its own block, then the block after; the first device along help never names the block before it, the last never the block after it. `tile_live`: on each device its live tiles come first; each device has two or more live tiles, and in every system one device has all 16 live.
All inputs are finite; a program needn't handle non-finite values.
Results may differ from a plain program's by a relative error of at most 0.0052.
Values may be sent and summed in bfloat16 or wider, within the bound.
A program may use at most 192 MiB of HBM per device.

v0:
```python
import jax
import jax.numpy as jnp
from jax import lax
from jax.experimental import pallas as pl
from jax.experimental.pallas import tpu as pltpu
from jax.sharding import PartitionSpec as P

MESH = pl.DeviceIdType.MESH
F32 = jnp.float32
BF16 = jnp.bfloat16

A = 64
NC = 9
C = 256
E = 1024
EB = 256
NB = E // EB
ROT = 35
TILE = 64
W9 = NC * C
ROWS = 9728
HALF = ROWS // 2
BLOCKS = ((0, 1, 0), (1, 3, 1), (10, 5, 4))
ORDER = (0, 2, 6, 3, 7, 1, 5, 8, 4)
POS = tuple(ORDER.index(c) for c in range(NC))
NATURAL = tuple(range(NC))
UNITS = (6, 6, 7)
START = (0, 1536, 3072)
AXES = (("x", "y", "z"), ("y", "z", "x"), ("z", "x", "y"))


def nn(a, b):
    return jnp.dot(a, b, preferred_element_type=F32)


def nt(a, b):
    return lax.dot_general(a, b, (((1,), (1,)), ((), ())), preferred_element_type=F32)


def eye(n):
    r = lax.broadcasted_iota(jnp.int32, (n, n), 0)
    c = lax.broadcasted_iota(jnp.int32, (n, n), 1)
    return jnp.where(r == c, 1.0, 0.0).astype(BF16)


def rotate(wide, work, in_pos, out, out_pos, lane0, inverse):
    for lt in range(EB // 128):
        lanes = pl.ds(lane0 + lt * 128, 128)
        for offset, extent, first in BLOCKS:
            d = [wide[offset + i, :, lanes][None] for i in range(extent * extent)]
            for chunk in range(0, C, 32):
                x = [
                    work[
                        pl.ds(in_pos[first + j] * C + chunk, 32), pl.ds(lt * 128, 128)
                    ].reshape(4, 8, 128)
                    for j in range(extent)
                ]
                for k in range(extent):
                    total = None
                    for j in range(extent):
                        entry = j * extent + k if inverse else k * extent + j
                        term = d[entry] * x[j]
                        total = term if total is None else total + term
                    out[pl.ds(out_pos[first + k] * C + chunk, 32), lanes] = total.reshape(
                        32, 128
                    ).astype(BF16)


def body(
    coef, cot, w0, w1, w2, src, tgt, rot, gate, live,
    upd, gco, O,
    hT, yT, X, T3, CT, cotT, W0T, M1f, M1b, M2f, M2b, wide, oh_s, oh_t,
    G, R0, S, R1, T1, R2, T2, R3, SB, RB,
    halo_s, halo_r, core_s, core_r, ring_s, ring_r,
):
    dp = lax.axis_index("dp")
    hp = lax.axis_index("help")
    x, core = dp // 2, dp % 2
    y, z = hp // 4, hp % 4
    at = {"x": x, "y": y, "z": z}

    def peer(axis, d):
        if axis == "x":
            return ((x + d) % 4 * 2 + core, hp)
        if axis == "y":
            return (dp, (y + d) % 4 * 4 + z)
        return (dp, y * 4 + (z + d) % 4)

    partner = (x * 2 + 1 - core, hp)
    above = (dp, (hp + 1) % 16)
    below = (dp, (hp + 15) % 16)

    barrier = pltpu.get_barrier_semaphore()
    peers = [partner, above, below] + [peer(a, d) for a in "xyz" for d in (1, 2, 3)]
    for device in peers:
        pl.semaphore_signal(barrier, inc=1, device_id=device, device_id_type=MESH)

    def remote(s, t, sem_s, sem_r, device):
        return pltpu.make_async_remote_copy(
            src_ref=s, dst_ref=t, send_sem=sem_s, recv_sem=sem_r,
            device_id=device, device_id_type=MESH,
        )

    halo = [
        remote(coef, T3.at[0], halo_s.at[0], halo_r.at[0], above),
        remote(coef, T3.at[1], halo_s.at[1], halo_r.at[1], below),
    ]
    give = [
        remote(SB.at[1], RB.at[0], halo_s.at[2], halo_r.at[2], above),
        remote(SB.at[0], RB.at[1], halo_s.at[3], halo_r.at[3], below),
    ]

    def half_rows(c):
        return pl.ds(pl.multiple_of(c * HALF, 256), HALF)

    swap = remote(G.at[half_rows(1 - core)], R0, core_s.at[0], core_r.at[0], partner)
    share = remote(
        O.at[half_rows(core)], O.at[half_rows(core)], core_s.at[1], core_r.at[1], partner
    )

    def ring(stage, make):
        return [
            [
                remote(*make(p, d), ring_s.at[stage, p, d - 1], ring_r.at[stage, p, d - 1], peer(AXES[p][(0, 1, 2, 1, 0)[stage]], d))
                for d in (1, 2, 3)
            ]
            for p in range(3)
        ]

    def first_make(p, d):
        q = UNITS[p] * 64
        j = (at[AXES[p][0]] + d) % 4
        return (
            S.at[pl.ds(pl.multiple_of(START[p] + j * q, 64), q)],
            R1.at[d - 1, pl.ds(START[p] // 4, q)],
        )

    def second_make(p, d):
        q = UNITS[p] * 16
        j = (at[AXES[p][1]] + d) % 4
        return (
            T1.at[pl.ds(pl.multiple_of(START[p] // 4 + j * q, 16), q)],
            R2.at[d - 1, pl.ds(START[p] // 16, q)],
        )

    def third_make(p, d):
        rows = pl.ds(START[p] // 16, UNITS[p] * 16)
        return T2.at[rows], R3.at[d - 1, rows]

    def place(p, deep):
        q = UNITS[p] * 16
        base = core * HALF + START[p] + at[AXES[p][0]] * (4 * q)
        if deep:
            return pl.ds(pl.multiple_of(base + at[AXES[p][1]] * q, 16), q)
        return pl.ds(pl.multiple_of(base, 64), 4 * q)

    def fourth_make(p, d):
        return O.at[place(p, True)], O.at[place(p, True)]

    def fifth_make(p, d):
        return O.at[place(p, False)], O.at[place(p, False)]

    stages = [
        ring(i, m)
        for i, m in enumerate((first_make, second_make, third_make, fourth_make, fifth_make))
    ]

    def start(stage):
        for part in stages[stage]:
            for copy in part:
                copy.start()

    def arrive(stage, p):
        for copy in stages[stage][p]:
            copy.wait_recv()

    wide[...] = jnp.broadcast_to(rot[...].astype(F32)[:, None, :], (ROT, 8, E))
    lane = lax.broadcasted_iota(jnp.int32, (1, E), 1) // TILE
    alive = jnp.zeros((1, E), F32)
    for t in range(E // TILE):
        alive = jnp.where(lane == t, live[0, t].astype(F32), alive)
    q = gate[...].astype(F32) * alive
    for r in range(0, 3 * A, A):
        ids = lax.broadcasted_iota(jnp.int32, (A, E), 0)
        oh_s[pl.ds(r, A), :] = jnp.where(ids + r == src[...], 1.0, 0.0).astype(BF16)
    ids = lax.broadcasted_iota(jnp.int32, (A, E), 0)
    oh_t[...] = jnp.where(ids == tgt[...], q, 0.0).astype(BF16)

    one = eye(C)
    for c in range(NC):
        cotT[pl.ds(c * C, C), :] = nt(one, cot[pl.ds(c * A, A), :]).astype(BF16)

    pl.semaphore_wait(barrier, len(peers))
    for copy in halo:
        copy.start()

    for i in range(3):
        W0T[pl.ds(i * C, C), :] = nt(one, w0[:, pl.ds(i * C, C)]).astype(BF16)
    for fwd, bwd, w, n in ((M1f, M1b, w1, 512), (M2f, M2b, w2, 256)):
        lo, hi = pl.ds(0, n), pl.ds(n, n)
        bwd[lo, lo] = w[0]
        bwd[lo, hi] = w[1]
        bwd[hi, lo] = -w[1]
        bwd[hi, hi] = w[0]
        for i in range(n // C):
            rows, next_rows = pl.ds(i * C, C), pl.ds(n + i * C, C)
            real = nt(one, w[0, :, pl.ds(i * C, C)])
            imag = nt(one, w[1, :, pl.ds(i * C, C)])
            fwd[rows, lo] = real.astype(BF16)
            fwd[rows, hi] = (-imag).astype(BF16)
            fwd[next_rows, lo] = imag.astype(BF16)
            fwd[next_rows, hi] = real.astype(BF16)

    def gather(table, onehot, out):
        def step(b, carry):
            lane0 = pl.multiple_of(b * EB, EB)
            pick = onehot[:, pl.ds(lane0, EB)]
            for c in range(NC):
                X[pl.ds(c * C, C), :] = nn(table[pl.ds(c * C, C), :], pick)
            rotate(wide, X, NATURAL, out, POS, lane0, False)
            return carry

        lax.fori_loop(0, NB, step, 0)

    gather(cotT, oh_t, hT)

    for copy in halo:
        copy.wait_recv()
    for c in range(NC):
        rows = pl.ds(c * A, A)
        both = jnp.concatenate([T3[0, rows, :], coef[rows, :], T3[1, rows, :]], axis=0)
        CT[pl.ds(c * C, C), :] = nt(one, both).astype(BF16)
    gather(CT, oh_s, yT)

    def put(base, col_rows, row0, value):
        for k in range(value.shape[1] // 128):
            G[pl.ds(base + k * col_rows + row0, value.shape[0]), :] = value[
                :, k * 128 : (k + 1) * 128
            ].astype(BF16)

    for i in range(3):
        for j in range(3):
            put(j * 2 * 768, 768, i * C, nt(yT[pl.ds(i * C, C), :], hT[pl.ds(j * C, C), :]))
    for base, a0, b0, n in ((4608, 768, 1280, 512), (8704, 1792, 2048, 256)):
        for i in range(n // C):
            ya, yb = yT[pl.ds(a0 + i * C, C), :], yT[pl.ds(b0 + i * C, C), :]
            for j in range(n // C):
                ha, hb = hT[pl.ds(a0 + j * C, C), :], hT[pl.ds(b0 + j * C, C), :]
                put(base + j * 2 * n, n, i * C, nt(ya, ha) + nt(yb, hb))
                put(base + n * n // 128 + j * 2 * n, n, i * C, nt(ya, hb) - nt(yb, ha))
    swap.start()

    def mix(zero, first, second, data, b):
        lane0 = pl.multiple_of(b * EB, EB)
        lanes = pl.ds(lane0, EB)
        for m, r0, n in ((zero, 0, 768), (first, 768, 1024), (second, 1792, 512)):
            right = data[pl.ds(r0, n), lanes]
            for i in range(n // C):
                X[pl.ds(r0 + i * C, C), :] = nn(m[pl.ds(i * C, C), :], right)
        rotate(wide, X, POS, data, NATURAL, lane0, True)

    def backward(lo, hi):
        lax.fori_loop(lo, hi, lambda b, t: (mix(w0, M1b, M2b, hT, b), t)[1], 0)

    def forward(lo, hi):
        lax.fori_loop(lo, hi, lambda b, t: (mix(W0T, M1f, M2f, yT, b), t)[1], 0)

    backward(0, 1)
    swap.wait_recv()

    def add_core(i, carry):
        rows = pl.ds(pl.multiple_of(i * 304, 16), 304)
        own = pl.ds(pl.multiple_of(core * HALF + i * 304, 16), 304)
        S[rows, :] = (G[own, :].astype(F32) + R0[rows, :].astype(F32)).astype(BF16)
        return carry

    lax.fori_loop(0, 16, add_core, 0)
    start(0)
    backward(1, 4)
    for c in range(NC):
        total = nt(oh_s[...], hT[pl.ds(c * C, C), :])
        rows = pl.ds(c * A, A)
        SB[0, rows, :] = total[0:A].astype(BF16)
        SB[1, rows, :] = total[2 * A : 3 * A].astype(BF16)
        X[rows, :] = total[A : 2 * A]
    for copy in give:
        copy.start()
    for p in range(3):
        arrive(0, p)
        n = UNITS[p] * 64
        own = pl.ds(pl.multiple_of(START[p] + at[AXES[p][0]] * n, 64), n)
        rows = pl.ds(START[p] // 4, n)
        T1[rows, :] = (S[own, :].astype(F32) + R1[1, rows, :].astype(F32)) + (
            R1[0, rows, :].astype(F32) + R1[2, rows, :].astype(F32)
        )
        for copy in stages[1][p]:
            copy.start()
    for copy in give:
        copy.wait_recv()
    gco[...] = (
        (cot[...].astype(F32) + X[pl.ds(0, NC * A), :])
        + (RB[0].astype(F32) + RB[1].astype(F32))
    ).astype(BF16)

    forward(0, 1)
    for p in range(3):
        arrive(1, p)
        n = UNITS[p] * 16
        own = pl.ds(pl.multiple_of(START[p] // 4 + at[AXES[p][1]] * n, 16), n)
        rows = pl.ds(START[p] // 16, n)
        T2[rows, :] = (T1[own, :] + R2[1, rows, :]) + (R2[0, rows, :] + R2[2, rows, :])
        for copy in stages[2][p]:
            copy.start()
    forward(1, 2)
    for p in range(3):
        arrive(2, p)
        rows = pl.ds(START[p] // 16, UNITS[p] * 16)
        O[place(p, True), :] = (
            (T2[rows, :] + R3[1, rows, :]) + (R3[0, rows, :] + R3[2, rows, :])
        ).astype(BF16)
        for copy in stages[3][p]:
            copy.start()
    forward(2, 3)
    for p in range(3):
        arrive(3, p)
        for copy in stages[4][p]:
            copy.start()
    forward(3, 4)
    for c in range(NC):
        rows = pl.ds(c * A, A)
        total = nt(oh_t[...], yT[pl.ds(c * C, C), :])
        upd[rows, :] = (coef[rows, :].astype(F32) + total).astype(BF16)
    for p in range(3):
        arrive(4, p)
    share.start()
    for copy in halo + give + [swap]:
        copy.wait_send()
    for stage in stages:
        for part in stage:
            for copy in part:
                copy.wait_send()
    share.wait()


def vmem(*shape):
    return pltpu.VMEM(shape, BF16)


def work(coef, cot, w0, w1, w2, src, tgt, rot, gate, live):
    whole = pl.BlockSpec(memory_space=pltpu.VMEM)
    return pl.pallas_call(
        body,
        out_shape=(
            jax.ShapeDtypeStruct((NC * A, C), BF16),
            jax.ShapeDtypeStruct((NC * A, C), BF16),
            jax.ShapeDtypeStruct((ROWS, 128), BF16),
        ),
        in_specs=[whole] * 9 + [pl.BlockSpec(memory_space=pltpu.SMEM)],
        out_specs=(whole,) * 3,
        scratch_shapes=[
            vmem(W9, E),
            vmem(W9, E),
            pltpu.VMEM((W9, EB), F32),
            vmem(2, NC * A, C),
            vmem(W9, 3 * A),
            vmem(W9, A),
            vmem(768, 768),
            vmem(1024, 1024),
            vmem(1024, 1024),
            vmem(512, 512),
            vmem(512, 512),
            pltpu.VMEM((ROT, 8, E), F32),
            vmem(3 * A, E),
            vmem(A, E),
            vmem(ROWS, 128),
            vmem(HALF, 128),
            vmem(HALF, 128),
            vmem(3, HALF // 4, 128),
            pltpu.VMEM((HALF // 4, 128), F32),
            pltpu.VMEM((3, HALF // 16, 128), F32),
            pltpu.VMEM((HALF // 16, 128), F32),
            pltpu.VMEM((3, HALF // 16, 128), F32),
            vmem(2, NC * A, C),
            vmem(2, NC * A, C),
            pltpu.SemaphoreType.DMA((4,)),
            pltpu.SemaphoreType.DMA((4,)),
            pltpu.SemaphoreType.DMA((2,)),
            pltpu.SemaphoreType.DMA((2,)),
            pltpu.SemaphoreType.DMA((5, 3, 3)),
            pltpu.SemaphoreType.DMA((5, 3, 3)),
        ],
        compiler_params=pltpu.CompilerParams(
            collective_id=0, has_side_effects=True, vmem_limit_bytes=56 * 2**20
        ),
        name="layer",
    )(coef, cot, w0, w1, w2, src, tgt, rot, gate, live)


def shards(coeffs, cotangent, w_zero, w_one, w_two, source, target, rotation, gate, tile_live):
    def by_coef(rows):
        return jnp.transpose(rows[0], (1, 0, 2)).reshape(NC * A, C)

    def by_atom(rows):
        return jnp.transpose(rows.reshape(NC, A, C), (1, 0, 2))[None]

    upd, gco, grads = work(
        by_coef(coeffs), by_coef(cotangent), w_zero, w_one, w_two,
        source, target, rotation[0], gate, tile_live,
    )
    zero = grads[:4608].reshape(6, 768, 128).transpose(1, 0, 2).reshape(768, 768)
    one = grads[4608:8704].reshape(2, 4, 512, 128).transpose(0, 2, 1, 3).reshape(2, 512, 512)
    two = grads[8704:].reshape(2, 2, 256, 128).transpose(0, 2, 1, 3).reshape(2, 256, 256)
    return by_atom(upd), by_atom(gco), zero.astype(F32), one.astype(F32), two.astype(F32)


def solution(mesh):
    return jax.shard_map(
        shards,
        mesh=mesh,
        in_specs=(
            P("dp", "help", None, None),
            P("dp", "help", None, None),
            P(),
            P(),
            P(),
            P("dp", "help"),
            P("dp", "help"),
            P("dp", None, "help"),
            P("dp", "help"),
            P("dp", "help"),
        ),
        out_specs=(P("dp", "help", None, None), P("dp", "help", None, None), P(), P(), P()),
        check_vma=False,
    )
```

profile of v0, /device:TPU:1, one launch (start us, length us, event | category | flops | bytes accessed | tf_op | source)
XLA Modules:
  0.0 84.1 jit_solution(8105243330557196739)
XLA Ops:
  0.6 73.4 %layer.1 = (bf16[576,256]{1,0:T(8,128)(2,1)}, bf16[576,256]{1,0:T(8,128)(2,1)}, bf16[9728,128]{1,0:T(8,128)(2,1)}) custom-call(bf16[576,256]{1,0:T(8,128)(2,1)} %bitcast.48, bf16[576,256]{1,0:T(8,128)(2,1)} %bitcast.49, bf16[768,768]{1,0:T(8,128)(2,1)} %w0.1, bf16[2,512,512]{2,1,0:T(8,128)(2,1)} %w1.1, bf16[2,256,256]{2,1,0:T(8,128)(2,1)} %w2.1, ...), custom_call_target="tpu_custom_call" | custom-call | tf_op jit(solution)/shard_map/layer/pallas_call | solution.py:351
  74.0 1.0 %slice.11 = bf16[1024,128]{1,0:T(8,128)(2,1)S(1)} slice(bf16[9728,128]{1,0:T(8,128)(2,1)} %get-tuple-element.10), slice={[8704:9728], [0:128]} | slice | bytes 524288 | tf_op jit(solution)/shard_map/slice | solution.py:412
  75.0 0.8 copy_bitcast_fusion.1
  75.8 1.3 %slice.10 = bf16[4096,128]{1,0:T(8,128)(2,1)S(1)} slice(bf16[9728,128]{1,0:T(8,128)(2,1)} %get-tuple-element.10), slice={[4608:8704], [0:128]} | slice | bytes 2097152 | tf_op jit(solution)/shard_map/slice | solution.py:411
  77.1 1.3 %slice.9 = bf16[4608,128]{1,0:T(8,128)(2,1)S(1)} slice(bf16[9728,128]{1,0:T(8,128)(2,1)} %get-tuple-element.10), slice={[0:4608], [0:128]} | slice | bytes 2359296 | tf_op jit(solution)/shard_map/slice | solution.py:410
  78.5 1.6 %copy_bitcast_fusion = f32[2,512,512]{2,1,0:T(8,128)} fusion(bf16[2,4,512,128]{3,2,1,0:T(8,128)(2,1)S(1)} %bitcast.44), kind=kLoop, calls=%fused_computation | loop fusion | flops 524288 | bytes 3145728 | tf_op jit(solution)/shard_map/convert_element_type | solution.py:413
  80.1 0.6 copy.18
  80.7 0.0 copy-start.1
  80.7 0.0 copy-start
  80.7 2.0 %copy.21 = f32[768,768]{1,0:T(8,128)} copy(f32[768,768]{0,1:T(8,128)S(1)} %bitcast.42) | data formatting | bytes 4718592
  82.7 0.0 copy-done.1
  82.7 0.7 copy.28
  83.4 0.0 copy-done
  83.4 0.7 copy.29
Async XLA Ops:
  80.7 2.0 %copy-start.1 = (bf16[576,256]{1,0:T(8,128)(2,1)S(1)}, bf16[576,256]{1,0:T(8,128)(2,1)}, u32[]{:S(2)}) copy-start(bf16[576,256]{1,0:T(8,128)(2,1)} %get-tuple-element.8) | copy-start | bytes 884740
  80.7 2.7 %copy-start = (bf16[576,256]{1,0:T(8,128)(2,1)S(1)}, bf16[576,256]{1,0:T(8,128)(2,1)}, u32[]{:S(2)}) copy-start(bf16[576,256]{1,0:T(8,128)(2,1)} %get-tuple-element.9) | copy-start | bytes 884740
where the time goes:
time: 84.3 us; the launch traced here: 84.1 us
  Pallas kernels  73.4 us (87%)
  local copies, waits for them, and re-layouts  7.59 us (9%)
  other arithmetic  2.43 us (3%)
    pallas_call x1, Pallas kernels, work(): pl.pallas_call(body, out_shape=(jax.ShapeDtypeStruct((NC * A, C), BF16),...  73.4 us
    unnamed x7, local copies, waits for them, and re-layouts  3.39 us

commit v1 on v0

v1 whole, which is shorter than its diff:
```python
import jax
import jax.numpy as jnp
from jax import lax
from jax.experimental import pallas as pl
from jax.experimental.pallas import tpu as pltpu
from jax.sharding import PartitionSpec as P

MESH = pl.DeviceIdType.MESH
F32 = jnp.float32
BF16 = jnp.bfloat16

A = 64
NC = 9
C = 256
E = 1024
EB = 256
NB = E // EB
ROT = 35
TILE = 64
W9 = NC * C
ROWS = 9728
HALF = ROWS // 2
BLOCKS = ((0, 1, 0), (1, 3, 1), (10, 5, 4))
ORDER = (0, 2, 6, 3, 7, 1, 5, 8, 4)
POS = tuple(ORDER.index(c) for c in range(NC))
NATURAL = tuple(range(NC))
UNITS = (6, 7, 6)
START = (0, 1536, 3328)
AXES = (("x", "y", "z"), ("y", "z", "x"), ("z", "x", "y"))


def nn(a, b):
    return jnp.dot(a, b, preferred_element_type=F32)


def nt(a, b):
    return lax.dot_general(a, b, (((1,), (1,)), ((), ())), preferred_element_type=F32)


def eye(n):
    r = lax.broadcasted_iota(jnp.int32, (n, n), 0)
    c = lax.broadcasted_iota(jnp.int32, (n, n), 1)
    return jnp.where(r == c, 1.0, 0.0).astype(BF16)


def rotate(wide, work, in_pos, out, out_pos, lane0, inverse, degrees=(0, 1, 2)):
    for lt in range(EB // 128):
        lanes = pl.ds(lane0 + lt * 128, 128)
        for offset, extent, first in [BLOCKS[g] for g in degrees]:
            d = [wide[offset + i, :, lanes][None] for i in range(extent * extent)]
            for chunk in range(0, C, 32):
                x = [
                    work[
                        pl.ds(in_pos[first + j] * C + chunk, 32), pl.ds(lt * 128, 128)
                    ].reshape(4, 8, 128)
                    for j in range(extent)
                ]
                for k in range(extent):
                    total = None
                    for j in range(extent):
                        entry = j * extent + k if inverse else k * extent + j
                        term = d[entry] * x[j]
                        total = term if total is None else total + term
                    out[pl.ds(out_pos[first + k] * C + chunk, 32), lanes] = total.reshape(
                        32, 128
                    ).astype(BF16)


def body(
    coef, cot, w0_in, w1_in, w2_in, src, tgt, rot, gate, live,
    upd, gco, O,
    w0, w1, w2, hT, yT, bT, X, own_sum, T3, CT, cotT, W0T, M1f, M1b, M2f, M2b, wide, oh_s, oh_t,
    G, R0, S, R1, T1, R2, T2, R3, SB, RB,
    halo_s, halo_r, core_s, core_r, ring_s, ring_r, load_sem,
):
    dp = lax.axis_index("dp")
    hp = lax.axis_index("help")
    x, core = dp // 2, dp % 2
    y, z = hp // 4, hp % 4
    at = {"x": x, "y": y, "z": z}

    def peer(axis, d):
        if axis == "x":
            return ((x + d) % 4 * 2 + core, hp)
        if axis == "y":
            return (dp, (y + d) % 4 * 4 + z)
        return (dp, y * 4 + (z + d) % 4)

    partner = (x * 2 + 1 - core, hp)
    above = (dp, (hp + 1) % 16)
    below = (dp, (hp + 15) % 16)

    barrier = pltpu.get_barrier_semaphore()
    peers = [partner, above, below] + [peer(a, d) for a in "xyz" for d in (1, 2, 3)]
    for device in peers:
        pl.semaphore_signal(barrier, inc=1, device_id=device, device_id_type=MESH)

    def remote(s, t, sem_s, sem_r, device):
        return pltpu.make_async_remote_copy(
            src_ref=s, dst_ref=t, send_sem=sem_s, recv_sem=sem_r,
            device_id=device, device_id_type=MESH,
        )

    halo = [
        [
            remote(coef.at[rows], T3.at[0, rows], halo_s.at[0, i], halo_r.at[0, i], above),
            remote(coef.at[rows], T3.at[1, rows], halo_s.at[1, i], halo_r.at[1, i], below),
        ]
        for i, rows in enumerate((pl.ds(0, 4 * A), pl.ds(4 * A, 5 * A)))
    ]
    give = [
        remote(SB.at[1], RB.at[0], halo_s.at[2, 0], halo_r.at[2, 0], above),
        remote(SB.at[0], RB.at[1], halo_s.at[2, 1], halo_r.at[2, 1], below),
    ]
    loads = [
        pltpu.make_async_copy(far, near, load_sem.at[i])
        for i, (far, near) in enumerate(((w0_in, w0), (w1_in, w1), (w2_in, w2)))
    ]
    for copy in loads:
        copy.start()

    swap = [
        remote(
            G.at[pl.ds(pl.multiple_of((1 - core) * HALF + START[p], 256), UNITS[p] * 256)],
            R0.at[pl.ds(START[p], UNITS[p] * 256)],
            core_s.at[4, p], core_r.at[4, p], partner,
        )
        for p in range(3)
    ]

    def quarter(p, d):
        n = UNITS[p] * 64
        row = core * HALF + START[p] + (at[AXES[p][0]] + 4 - d) % 4 * n
        return O.at[pl.ds(pl.multiple_of(row, 64), n)]

    share = [
        [
            remote(quarter(p, d), quarter(p, d), core_s.at[d, p], core_r.at[d, p], partner)
            for d in range(4)
        ]
        for p in range(3)
    ]

    def ring(stage, make):
        return [
            [
                remote(*make(p, d), ring_s.at[stage, p, d - 1], ring_r.at[stage, p, d - 1], peer(AXES[p][(0, 1, 2, 1, 0)[stage]], d))
                for d in (1, 2, 3)
            ]
            for p in range(3)
        ]

    def first_make(p, d):
        q = UNITS[p] * 64
        j = (at[AXES[p][0]] + d) % 4
        return (
            S.at[pl.ds(pl.multiple_of(START[p] + j * q, 64), q)],
            R1.at[d - 1, pl.ds(START[p] // 4, q)],
        )

    def second_make(p, d):
        q = UNITS[p] * 16
        j = (at[AXES[p][1]] + d) % 4
        return (
            T1.at[pl.ds(pl.multiple_of(START[p] // 4 + j * q, 16), q)],
            R2.at[d - 1, pl.ds(START[p] // 16, q)],
        )

    def third_make(p, d):
        rows = pl.ds(START[p] // 16, UNITS[p] * 16)
        return T2.at[rows], R3.at[d - 1, rows]

    def place(p, deep):
        q = UNITS[p] * 16
        base = core * HALF + START[p] + at[AXES[p][0]] * (4 * q)
        if deep:
            return pl.ds(pl.multiple_of(base + at[AXES[p][1]] * q, 16), q)
        return pl.ds(pl.multiple_of(base, 64), 4 * q)

    def fourth_make(p, d):
        return O.at[place(p, True)], O.at[place(p, True)]

    def fifth_make(p, d):
        return O.at[place(p, False)], O.at[place(p, False)]

    stages = [
        ring(i, m)
        for i, m in enumerate((first_make, second_make, third_make, fourth_make, fifth_make))
    ]

    def go(stage, p):
        for copy in stages[stage][p]:
            copy.start()

    def arrive(stage, p):
        for copy in stages[stage][p]:
            copy.wait_recv()

    def advance(k, p):
        n = UNITS[p] * 64
        if k == 0:
            swap[p].wait_recv()

            def add_core(i, carry):
                rows = pl.ds(pl.multiple_of(START[p] + i * n, 64), n)
                own = pl.ds(pl.multiple_of(core * HALF + START[p] + i * n, 64), n)
                S[rows, :] = (G[own, :].astype(F32) + R0[rows, :].astype(F32)).astype(BF16)
                return carry

            lax.fori_loop(0, 4, add_core, 0)
            go(0, p)
        elif k == 1:
            arrive(0, p)
            own = pl.ds(pl.multiple_of(START[p] + at[AXES[p][0]] * n, 64), n)
            rows = pl.ds(START[p] // 4, n)
            T1[rows, :] = (S[own, :].astype(F32) + R1[1, rows, :].astype(F32)) + (
                R1[0, rows, :].astype(F32) + R1[2, rows, :].astype(F32)
            )
            go(1, p)
        elif k == 2:
            arrive(1, p)
            n = n // 4
            own = pl.ds(pl.multiple_of(START[p] // 4 + at[AXES[p][1]] * n, 16), n)
            rows = pl.ds(START[p] // 16, n)
            T2[rows, :] = (T1[own, :] + R2[1, rows, :]) + (R2[0, rows, :] + R2[2, rows, :])
            go(2, p)
        elif k == 3:
            arrive(2, p)
            rows = pl.ds(START[p] // 16, n // 4)
            O[place(p, True), :] = (
                (T2[rows, :] + R3[1, rows, :]) + (R3[0, rows, :] + R3[2, rows, :])
            ).astype(BF16)
            go(3, p)
        elif k == 4:
            arrive(3, p)
            go(4, p)
            share[p][0].start()
        else:
            for d in (1, 2, 3):
                stages[4][p][d - 1].wait_recv()
                share[p][d].start()

    wide[...] = jnp.broadcast_to(rot[...].astype(F32)[:, None, :], (ROT, 8, E))
    lane = lax.broadcasted_iota(jnp.int32, (1, E), 1) // TILE
    alive = jnp.zeros((1, E), F32)
    for t in range(E // TILE):
        alive = jnp.where(lane == t, live[0, t].astype(F32), alive)
    q = gate[...].astype(F32) * alive
    for r in range(0, 3 * A, A):
        ids = lax.broadcasted_iota(jnp.int32, (A, E), 0)
        oh_s[pl.ds(r, A), :] = jnp.where(ids + r == src[...], 1.0, 0.0).astype(BF16)
    ids = lax.broadcasted_iota(jnp.int32, (A, E), 0)
    oh_t[...] = jnp.where(ids == tgt[...], q, 0.0).astype(BF16)

    pl.semaphore_wait(barrier, len(peers))
    for pair in halo:
        for copy in pair:
            copy.start()

    one = eye(C)
    for c in range(NC):
        cotT[pl.ds(c * C, C), :] = nt(one, cot[pl.ds(c * A, A), :]).astype(BF16)
    for copy in loads:
        copy.wait()
    for i in range(3):
        W0T[pl.ds(i * C, C), :] = nt(one, w0[:, pl.ds(i * C, C)]).astype(BF16)
    for fwd, bwd, w, n in ((M1f, M1b, w1, 512), (M2f, M2b, w2, 256)):
        lo, hi = pl.ds(0, n), pl.ds(n, n)
        bwd[lo, lo] = w[0]
        bwd[lo, hi] = w[1]
        bwd[hi, lo] = -w[1]
        bwd[hi, hi] = w[0]
        for i in range(n // C):
            rows, next_rows = pl.ds(i * C, C), pl.ds(n + i * C, C)
            real = nt(one, w[0, :, pl.ds(i * C, C)])
            imag = nt(one, w[1, :, pl.ds(i * C, C)])
            fwd[rows, lo] = real.astype(BF16)
            fwd[rows, hi] = (-imag).astype(BF16)
            fwd[next_rows, lo] = imag.astype(BF16)
            fwd[next_rows, hi] = real.astype(BF16)

    def gather(table, onehot, out, degrees):
        def step(b, carry):
            lane0 = pl.multiple_of(b * EB, EB)
            pick = onehot[:, pl.ds(lane0, EB)]
            for g in degrees:
                for c in range(g * g, (g + 1) * (g + 1)):
                    X[pl.ds(c * C, C), :] = nn(table[pl.ds(c * C, C), :], pick)
                rotate(wide, X, NATURAL, out, POS, lane0, False, (g,))
            return carry

        lax.fori_loop(0, NB, step, 0)

    def mix(zero, first, second, data, out, b):
        lane0 = pl.multiple_of(b * EB, EB)
        lanes = pl.ds(lane0, EB)
        for m, r0, n in ((zero, 0, 768), (first, 768, 1024), (second, 1792, 512)):
            right = data[pl.ds(r0, n), lanes]
            for i in range(n // C):
                X[pl.ds(r0 + i * C, C), :] = nn(m[pl.ds(i * C, C), :], right)
        rotate(wide, X, POS, out, NATURAL, lane0, True)

    def backward(lo, hi):
        lax.fori_loop(lo, hi, lambda b, t: (mix(w0, M1b, M2b, hT, bT, b), t)[1], 0)

    def forward(lo, hi):
        lax.fori_loop(lo, hi, lambda b, t: (mix(W0T, M1f, M2f, yT, yT, b), t)[1], 0)

    gather(cotT, oh_t, hT, (0, 1, 2))
    backward(0, 1)

    def table(i, coefs):
        for copy in halo[i]:
            copy.wait_recv()
        for c in coefs:
            rows = pl.ds(c * A, A)
            both = jnp.concatenate([T3[0, rows, :], coef[rows, :], T3[1, rows, :]], axis=0)
            CT[pl.ds(c * C, C), :] = nt(one, both).astype(BF16)

    def put(tile, value):
        for k in range(2):
            G[pl.ds(k * HALF + tile * C, C), :] = value[:, k * 128 : (k + 1) * 128].astype(BF16)

    def zero_tiles(tile, i):
        for j in range(3):
            put(tile + j, nt(yT[pl.ds(i * C, C), :], hT[pl.ds(j * C, C), :]))

    def pair_tiles(tile, a0, b0, n, i):
        ya, yb = yT[pl.ds(a0 + i * C, C), :], yT[pl.ds(b0 + i * C, C), :]
        for j in range(n):
            ha, hb = hT[pl.ds(a0 + j * C, C), :], hT[pl.ds(b0 + j * C, C), :]
            put(tile + j, nt(ya, ha) + nt(yb, hb))
            put(tile + n + j, nt(ya, hb) - nt(yb, ha))

    table(0, range(4))
    gather(CT, oh_s, yT, (0, 1))
    zero_tiles(0, 0)
    zero_tiles(3, 1)
    swap[0].start()
    pair_tiles(6, 768, 1280, 2, 0)
    table(1, range(4, 9))
    gather(CT, oh_s, yT, (2,))
    advance(0, 0)
    zero_tiles(10, 2)
    swap[1].start()
    pair_tiles(13, 768, 1280, 2, 1)
    pair_tiles(17, 1792, 2048, 1, 0)
    swap[2].start()
    advance(0, 1)
    backward(1, 2)
    advance(0, 2)
    advance(1, 0)
    backward(2, 4)
    advance(1, 1)

    def sum_back(coefs):
        for c in coefs:
            total = nt(oh_s[...], bT[pl.ds(c * C, C), :])
            rows = pl.ds(c * A, A)
            SB[0, rows, :] = total[0:A].astype(BF16)
            SB[1, rows, :] = total[2 * A : 3 * A].astype(BF16)
            own_sum[rows, :] = total[A : 2 * A]

    sum_back(range(5))
    advance(2, 0)
    advance(1, 2)
    sum_back(range(5, 9))
    for copy in give:
        copy.start()
    forward(0, 1)
    advance(2, 1)
    advance(3, 0)
    forward(1, 2)
    advance(2, 2)
    forward(2, 3)
    advance(3, 1)
    advance(4, 0)
    forward(3, 4)
    advance(3, 2)
    advance(4, 1)
    for c in range(NC):
        rows = pl.ds(c * A, A)
        total = nt(oh_t[...], yT[pl.ds(c * C, C), :])
        upd[rows, :] = (coef[rows, :].astype(F32) + total).astype(BF16)
    for copy in give:
        copy.wait_recv()
    gco[...] = (
        (cot[...].astype(F32) + own_sum[...]) + (RB[0].astype(F32) + RB[1].astype(F32))
    ).astype(BF16)
    advance(5, 0)
    advance(4, 2)
    advance(5, 1)
    advance(5, 2)
    for copy in halo[0] + halo[1] + give + swap:
        copy.wait_send()
    for stage in stages:
        for part in stage:
            for copy in part:
                copy.wait_send()
    for part in share:
        for copy in part:
            copy.wait()


def finish(upd, gco, O, upd_out, gco_out, g_zero, g_one, g_two):
    upd_out[...] = upd[...]
    gco_out[...] = gco[...]

    def tile(t, out, row, col):
        for k in range(2):
            out[pl.ds(row * C, C), pl.ds(col * C + k * 128, 128)] = O[
                pl.ds(k * HALF + t * C, C), :
            ].astype(F32)

    for j in range(3):
        for i, t in enumerate((0, 3, 10)):
            tile(t + j, g_zero, i, j)
    for part in range(2):
        for j in range(2):
            for i, t in enumerate((6, 13)):
                tile(t + 2 * part + j, g_one.at[part], i, j)
        tile(17 + part, g_two.at[part], 0, 0)


def vmem(*shape):
    return pltpu.VMEM(shape, BF16)


def work(coef, cot, w0, w1, w2, src, tgt, rot, gate, live):
    whole = pl.BlockSpec(memory_space=pltpu.VMEM)
    return pl.pallas_call(
        body,
        out_shape=(
            jax.ShapeDtypeStruct((NC * A, C), BF16),
            jax.ShapeDtypeStruct((NC * A, C), BF16),
            jax.ShapeDtypeStruct((ROWS, 128), BF16),
        ),
        in_specs=[whole] * 2
        + [pl.BlockSpec(memory_space=pl.ANY)] * 3
        + [whole] * 4
        + [pl.BlockSpec(memory_space=pltpu.SMEM)],
        out_specs=(whole,) * 3,
        scratch_shapes=[
            vmem(768, 768),
            vmem(2, 512, 512),
            vmem(2, 256, 256),
            vmem(W9, E),
            vmem(W9, E),
            vmem(W9, E),
            pltpu.VMEM((W9, EB), F32),
            pltpu.VMEM((NC * A, C), F32),
            vmem(2, NC * A, C),
            vmem(W9, 3 * A),
            vmem(W9, A),
            vmem(768, 768),
            vmem(1024, 1024),
            vmem(1024, 1024),
            vmem(512, 512),
            vmem(512, 512),
            pltpu.VMEM((ROT, 8, E), F32),
            vmem(3 * A, E),
            vmem(A, E),
            vmem(ROWS, 128),
            vmem(HALF, 128),
            vmem(HALF, 128),
            vmem(3, HALF // 4, 128),
            pltpu.VMEM((HALF // 4, 128), F32),
            pltpu.VMEM((3, HALF // 16, 128), F32),
            pltpu.VMEM((HALF // 16, 128), F32),
            pltpu.VMEM((3, HALF // 16, 128), F32),
            vmem(2, NC * A, C),
            vmem(2, NC * A, C),
            pltpu.SemaphoreType.DMA((3, 2)),
            pltpu.SemaphoreType.DMA((3, 2)),
            pltpu.SemaphoreType.DMA((5, 3)),
            pltpu.SemaphoreType.DMA((5, 3)),
            pltpu.SemaphoreType.DMA((5, 3, 3)),
            pltpu.SemaphoreType.DMA((5, 3, 3)),
            pltpu.SemaphoreType.DMA((3,)),
        ],
        compiler_params=pltpu.CompilerParams(
            collective_id=0, has_side_effects=True, vmem_limit_bytes=56 * 2**20
        ),
        name="layer",
    )(coef, cot, w0, w1, w2, src, tgt, rot, gate, live)


def shards(coeffs, cotangent, w_zero, w_one, w_two, source, target, rotation, gate, tile_live):
    def by_coef(rows):
        return jnp.transpose(rows[0], (1, 0, 2)).reshape(NC * A, C)

    def by_atom(rows):
        return jnp.transpose(rows.reshape(NC, A, C), (1, 0, 2))[None]

    upd, gco, grads = work(
        by_coef(coeffs), by_coef(cotangent), w_zero, w_one, w_two,
        source, target, rotation[0], gate, tile_live,
    )
    whole = pl.BlockSpec(memory_space=pltpu.VMEM)
    upd, gco, zero, one, two = pl.pallas_call(
        finish,
        out_shape=(
            jax.ShapeDtypeStruct((NC * A, C), BF16),
            jax.ShapeDtypeStruct((NC * A, C), BF16),
            jax.ShapeDtypeStruct((768, 768), F32),
            jax.ShapeDtypeStruct((2, 512, 512), F32),
            jax.ShapeDtypeStruct((2, 256, 256), F32),
        ),
        in_specs=[whole] * 3,
        out_specs=(whole,) * 5,
        compiler_params=pltpu.CompilerParams(vmem_limit_bytes=24 * 2**20),
        name="finish",
    )(upd, gco, grads)
    return by_atom(upd), by_atom(gco), zero, one, two


def solution(mesh):
    return jax.shard_map(
        shards,
        mesh=mesh,
        in_specs=(
            P("dp", "help", None, None),
            P("dp", "help", None, None),
            P(),
            P(),
            P(),
            P("dp", "help"),
            P("dp", "help"),
            P("dp", None, "help"),
            P("dp", "help"),
            P("dp", "help"),
        ),
        out_specs=(P("dp", "help", None, None), P("dp", "help", None, None), P(), P(), P()),
        check_vma=False,
    )
```

time: 84.3 us -> 76.4 us (0.906)
  local copies, waits for them, and re-layouts: 7.59 us -> 3.62 us
  other arithmetic: 2.43 us -> 0 us
  Pallas kernels: 73.4 us -> 71.9 us
    pallas_call x1, Pallas kernels: 73.4 us -> 69 us  [work(): pl.pallas_call(body, out_shape=(jax.ShapeDtypeStruct((NC * A, C), BF16),...]
    slice x3 -> x0, local copies, waits for them, and re-layouts: 3.61 us -> none  [the longest x1 1.35 us: shards(): grads[:4608].reshape(6, 768, 128).transpose(1, 0, 2).reshape(768, 768)]
    pallas_call x0 -> x1, Pallas kernels: none -> 2.84 us  [shards(): pl.pallas_call(finish, out_shape=(jax.ShapeDtypeStruct((NC * A, C), BF16)...]
    convert_element_type x2 -> x0, other arithmetic: 2.43 us -> none  [the longest x1 1.6 us: shards(): one.astype(F32)]
    unnamed x7 -> x6, local copies, waits for them, and re-layouts: 3.39 us -> 3.62 us
where the time goes in v1:
time: 76.4 us; the launch traced here: 76.2 us
  Pallas kernels  71.9 us (94%)
  local copies, waits for them, and re-layouts  3.62 us (5%)
    pallas_call x1, Pallas kernels, work(): pl.pallas_call(body, out_shape=(jax.ShapeDtypeStruct((NC * A, C), BF16),...  69 us
    unnamed x6, local copies, waits for them, and re-layouts  3.62 us
    pallas_call x1, Pallas kernels, shards(): pl.pallas_call(finish, out_shape=(jax.ShapeDtypeStruct((NC * A, C), BF16)...  2.84 us

profile of v1, /device:TPU:1, one launch (start us, length us, event | category | flops | bytes accessed | tf_op | source)
XLA Modules:
  0.0 76.2 jit_solution(7698225363979512844)
XLA Ops:
  0.6 69.0 %layer.1 = (bf16[576,256]{1,0:T(8,128)(2,1)}, bf16[576,256]{1,0:T(8,128)(2,1)}, bf16[9728,128]{1,0:T(8,128)(2,1)}) custom-call(bf16[576,256]{1,0:T(8,128)(2,1)} %bitcast.21, bf16[576,256]{1,0:T(8,128)(2,1)} %bitcast.22, bf16[768,768]{1,0:T(8,128)(2,1)} %w0_in.1, bf16[2,512,512]{2,1,0:T(8,128)(2,1)} %w1_in.1, bf16[2,256,256]{2,1,0:T(8,128)(2,1)} %w2_in.1, ...), custom_call_target="tpu_custom_call" | custom-call | tf_op jit(solution)/shard_map/layer/pallas_call | solution.py:431
  69.7 0.0 copy-start
  69.7 1.7 %copy-done = bf16[9728,128]{1,0:T(8,128)(2,1)S(1)} copy-done((bf16[9728,128]{1,0:T(8,128)(2,1)S(1)}, bf16[9728,128]{1,0:T(8,128)(2,1)}, u32[]{:S(2)}) %copy-start) | copy-done | bytes 2490392
  71.4 0.0 copy-start.1
  71.4 1.0 %copy-done.1 = bf16[576,256]{1,0:T(8,128)(2,1)S(1)} copy-done((bf16[576,256]{1,0:T(8,128)(2,1)S(1)}, bf16[576,256]{1,0:T(8,128)(2,1)}, u32[]{:S(2)}) %copy-start.1) | copy-done | bytes 294936
  72.3 0.0 copy-start.2
  72.3 1.0 %copy-done.2 = bf16[576,256]{1,0:T(8,128)(2,1)S(1)} copy-done((bf16[576,256]{1,0:T(8,128)(2,1)S(1)}, bf16[576,256]{1,0:T(8,128)(2,1)}, u32[]{:S(2)}) %copy-start.2) | copy-done | bytes 294936
  73.3 2.8 %finish.1 = (bf16[576,256]{1,0:T(8,128)(2,1)}, bf16[576,256]{1,0:T(8,128)(2,1)}, f32[768,768]{1,0:T(8,128)}, f32[2,512,512]{2,1,0:T(8,128)}, f32[2,256,256]{2,1,0:T(8,128)}) custom-call(bf16[576,256]{1,0:T(8,128)(2,1)S(1)} %copy-done.1, bf16[576,256]{1,0:T(8,128)(2,1)S(1)} %copy-done.2, bf16[9728,128]{1,0:T(8,128)(2,1)S(1)} %copy-done), custom_call_target="tpu_custom_call" | custom-call | tf_op jit(solution)/shard_map/finish/pallas_call | solution.py:500
Async XLA Ops:
  69.7 1.7 %copy-start = (bf16[9728,128]{1,0:T(8,128)(2,1)S(1)}, bf16[9728,128]{1,0:T(8,128)(2,1)}, u32[]{:S(2)}) copy-start(bf16[9728,128]{1,0:T(8,128)(2,1)} %get-tuple-element.15.O) | copy-start | bytes 7471108
  71.4 1.0 %copy-start.1 = (bf16[576,256]{1,0:T(8,128)(2,1)S(1)}, bf16[576,256]{1,0:T(8,128)(2,1)}, u32[]{:S(2)}) copy-start(bf16[576,256]{1,0:T(8,128)(2,1)} %get-tuple-element.13.upd) | copy-start | bytes 884740
  72.3 1.0 %copy-start.2 = (bf16[576,256]{1,0:T(8,128)(2,1)S(1)}, bf16[576,256]{1,0:T(8,128)(2,1)}, u32[]{:S(2)}) copy-start(bf16[576,256]{1,0:T(8,128)(2,1)} %get-tuple-element.14.gco) | copy-start | bytes 884740

commit v2 on v1

--- a/solution.py
+++ b/solution.py
@@ -67,11 +67,11 @@
 
 
 def body(
-    coef, cot, w0_in, w1_in, w2_in, src, tgt, rot, gate, live,
-    upd, gco, O,
-    w0, w1, w2, hT, yT, bT, X, own_sum, T3, CT, cotT, W0T, M1f, M1b, M2f, M2b, wide, oh_s, oh_t,
+    coef_in, cot_in, w0_in, w1_in, w2_in, rot_in, src, tgt, gate, live,
+    upd_out, gco_out, O_out,
+    coef, cot, rot, upd, gco, O, w0, w1, w2, hT, yT, bT, X, own_sum, T3, CT, cotT, W0T, M1f, M1b, M2f, M2b, wide, oh_s, oh_t,
     G, R0, S, R1, T1, R2, T2, R3, SB, RB,
-    halo_s, halo_r, core_s, core_r, ring_s, ring_r, load_sem,
+    halo_s, halo_r, core_s, core_r, ring_s, ring_r, load_sem, store_sem,
 ):
     dp = lax.axis_index("dp")
     hp = lax.axis_index("help")
@@ -103,21 +103,39 @@
 
     halo = [
         [
-            remote(coef.at[rows], T3.at[0, rows], halo_s.at[0, i], halo_r.at[0, i], above),
-            remote(coef.at[rows], T3.at[1, rows], halo_s.at[1, i], halo_r.at[1, i], below),
+            remote(coef_in.at[rows], T3.at[0, rows], halo_s.at[0, i], halo_r.at[0, i], above),
+            remote(coef_in.at[rows], T3.at[1, rows], halo_s.at[1, i], halo_r.at[1, i], below),
         ]
         for i, rows in enumerate((pl.ds(0, 4 * A), pl.ds(4 * A, 5 * A)))
     ]
     give = [
-        remote(SB.at[1], RB.at[0], halo_s.at[2, 0], halo_r.at[2, 0], above),
-        remote(SB.at[0], RB.at[1], halo_s.at[2, 1], halo_r.at[2, 1], below),
+        [
+            remote(SB.at[1, rows], RB.at[0, rows], halo_s.at[0, i], halo_r.at[0, i], above),
+            remote(SB.at[0, rows], RB.at[1, rows], halo_s.at[1, i], halo_r.at[1, i], below),
+        ]
+        for i, rows in ((2 + i, pl.ds(3 * A * i, 3 * A)) for i in range(3))
     ]
     loads = [
         pltpu.make_async_copy(far, near, load_sem.at[i])
-        for i, (far, near) in enumerate(((w0_in, w0), (w1_in, w1), (w2_in, w2)))
+        for i, (far, near) in enumerate(
+            ((cot_in, cot), (rot_in, rot), (coef_in, coef), (w0_in, w0), (w1_in, w1), (w2_in, w2))
+        )
     ]
     for copy in loads:
         copy.start()
+
+    def stored(half, p):
+        rows = pl.ds(pl.multiple_of(half * HALF + START[p], 256), UNITS[p] * 256)
+        return O.at[rows], O_out.at[rows]
+
+    stores = [
+        pltpu.make_async_copy(*pair, store_sem.at[i])
+        for i, pair in enumerate(
+            [stored(core, p) for p in range(3)]
+            + [stored(1 - core, p) for p in range(3)]
+            + [(upd, upd_out), (gco, gco_out)]
+        )
+    ]
 
     swap = [
         remote(
@@ -239,7 +257,15 @@
             for d in (1, 2, 3):
                 stages[4][p][d - 1].wait_recv()
                 share[p][d].start()
-
+            stores[p].start()
+
+    pl.semaphore_wait(barrier, len(peers))
+    for pair in halo:
+        for copy in pair:
+            copy.start()
+
+    loads[0].wait()
+    loads[1].wait()
     wide[...] = jnp.broadcast_to(rot[...].astype(F32)[:, None, :], (ROT, 8, E))
     lane = lax.broadcasted_iota(jnp.int32, (1, E), 1) // TILE
     alive = jnp.zeros((1, E), F32)
@@ -252,15 +278,10 @@
     ids = lax.broadcasted_iota(jnp.int32, (A, E), 0)
     oh_t[...] = jnp.where(ids == tgt[...], q, 0.0).astype(BF16)
 
-    pl.semaphore_wait(barrier, len(peers))
-    for pair in halo:
-        for copy in pair:
-            copy.start()
-
     one = eye(C)
     for c in range(NC):
         cotT[pl.ds(c * C, C), :] = nt(one, cot[pl.ds(c * A, A), :]).astype(BF16)
-    for copy in loads:
+    for copy in loads[2:]:
         copy.wait()
     for i in range(3):
         W0T[pl.ds(i * C, C), :] = nt(one, w0[:, pl.ds(i * C, C)]).astype(BF16)
@@ -361,17 +382,22 @@
             SB[1, rows, :] = total[2 * A : 3 * A].astype(BF16)
             own_sum[rows, :] = total[A : 2 * A]
 
-    sum_back(range(5))
+    sum_back(range(3))
     advance(2, 0)
     advance(1, 2)
-    sum_back(range(5, 9))
-    for copy in give:
+    for copy in give[0]:
         copy.start()
+    sum_back(range(3, 6))
     forward(0, 1)
     advance(2, 1)
     advance(3, 0)
+    for copy in give[1]:
+        copy.start()
+    sum_back(range(6, 9))
+    advance(2, 2)
+    for copy in give[2]:
+        copy.start()
     forward(1, 2)
-    advance(2, 2)
     forward(2, 3)
     advance(3, 1)
     advance(4, 0)
@@ -382,52 +408,75 @@
         rows = pl.ds(c * A, A)
         total = nt(oh_t[...], yT[pl.ds(c * C, C), :])
         upd[rows, :] = (coef[rows, :].astype(F32) + total).astype(BF16)
-    for copy in give:
-        copy.wait_recv()
+    stores[6].start()
+    advance(4, 2)
+    for pair in give:
+        for copy in pair:
+            copy.wait_recv()
     gco[...] = (
         (cot[...].astype(F32) + own_sum[...]) + (RB[0].astype(F32) + RB[1].astype(F32))
     ).astype(BF16)
-    advance(5, 0)
-    advance(4, 2)
-    advance(5, 1)
-    advance(5, 2)
-    for copy in halo[0] + halo[1] + give + swap:
-        copy.wait_send()
-    for stage in stages:
-        for part in stage:
-            for copy in part:
-                copy.wait_send()
-    for part in share:
-        for copy in part:
-            copy.wait()
-
-
-def finish(upd, gco, O, upd_out, gco_out, g_zero, g_one, g_two):
-    upd_out[...] = upd[...]
-    gco_out[...] = gco[...]
-
-    def tile(t, out, row, col):
-        for k in range(2):
-            out[pl.ds(row * C, C), pl.ds(col * C + k * 128, 128)] = O[
-                pl.ds(k * HALF + t * C, C), :
-            ].astype(F32)
-
-    for j in range(3):
-        for i, t in enumerate((0, 3, 10)):
-            tile(t + j, g_zero, i, j)
-    for part in range(2):
-        for j in range(2):
-            for i, t in enumerate((6, 13)):
-                tile(t + 2 * part + j, g_one.at[part], i, j)
-        tile(17 + part, g_two.at[part], 0, 0)
+    stores[7].start()
+    for p in range(3):
+        advance(5, p)
+    for p in range(3):
+        for copy in share[p]:
+            copy.wait_recv()
+        stores[3 + p].start()
+    for group in (*halo, *give, swap, *share, *(part for stage in stages for part in stage)):
+        for copy in group:
+            copy.wait_send()
+    for copy in stores:
+        copy.wait()
+
+
+RUNS = ((0, 3, 0, 0), (3, 3, 0, 1), (6, 4, 1, 0), (10, 3, 0, 2), (13, 4, 1, 1), (17, 2, 2, 0))
+
+
+def finish(upd, gco, O, upd_out, gco_out, g_zero, g_one, g_two, near, zero, one, two, sem):
+    count = len(RUNS)
+    straight = [
+        pltpu.make_async_copy(upd, upd_out, sem.at[3 * count]),
+        pltpu.make_async_copy(gco, gco_out, sem.at[3 * count + 1]),
+    ]
+    reads = []
+    for i, (t, n, _, _) in enumerate(RUNS):
+        rows = pl.ds(t * C, n * C)
+        reads.append(pltpu.make_async_copy(O.at[:, rows], near.at[:, rows], sem.at[i]))
+    for copy in reads + straight:
+        copy.start()
+    writes = []
+    for i, (t, n, kind, row) in enumerate(RUNS):
+        reads[i].wait()
+        rows = pl.ds(row * C, C)
+        parts = ((zero, g_zero),) if kind == 0 else ((one, g_one), (two, g_two))[kind - 1 : kind]
+        held, far = parts[0]
+        for part in range(1 if kind == 0 else 2):
+            block = held if kind == 0 else held.at[part]
+            width = n if kind == 0 else n // 2
+            for j in range(width):
+                for k in range(2):
+                    block[rows, pl.ds(j * C + k * 128, 128)] = near[
+                        k, pl.ds((t + part * width + j) * C, C), :
+                    ].astype(F32)
+            write = pltpu.make_async_copy(
+                block.at[rows],
+                (far if kind == 0 else far.at[part]).at[rows],
+                sem.at[count + 2 * i + part],
+            )
+            write.start()
+            writes.append(write)
+    for copy in straight + writes:
+        copy.wait()
 
 
 def vmem(*shape):
     return pltpu.VMEM(shape, BF16)
 
 
-def work(coef, cot, w0, w1, w2, src, tgt, rot, gate, live):
+def work(coef, cot, w0, w1, w2, rot, src, tgt, gate, live):
     whole = pl.BlockSpec(memory_space=pltpu.VMEM)
+    far = pl.BlockSpec(memory_space=pltpu.HBM)
     return pl.pallas_call(
         body,
         out_shape=(
@@ -435,12 +484,15 @@
             jax.ShapeDtypeStruct((NC * A, C), BF16),
             jax.ShapeDtypeStruct((ROWS, 128), BF16),
         ),
-        in_specs=[whole] * 2
-        + [pl.BlockSpec(memory_space=pl.ANY)] * 3
-        + [whole] * 4
-        + [pl.BlockSpec(memory_space=pltpu.SMEM)],
-        out_specs=(whole,) * 3,
+        in_specs=[far] * 6 + [whole] * 3 + [pl.BlockSpec(memory_space=pltpu.SMEM)],
+        out_specs=(far,) * 3,
         scratch_shapes=[
+            vmem(NC * A, C),
+            vmem(NC * A, C),
+            vmem(ROT, E),
+            vmem(NC * A, C),
+            vmem(NC * A, C),
+            vmem(ROWS, 128),
             vmem(768, 768),
             vmem(2, 512, 512),
             vmem(2, 256, 256),
@@ -470,19 +522,20 @@
             pltpu.VMEM((3, HALF // 16, 128), F32),
             vmem(2, NC * A, C),
             vmem(2, NC * A, C),
-            pltpu.SemaphoreType.DMA((3, 2)),
-            pltpu.SemaphoreType.DMA((3, 2)),
+            pltpu.SemaphoreType.DMA((2, 5)),
+            pltpu.SemaphoreType.DMA((2, 5)),
             pltpu.SemaphoreType.DMA((5, 3)),
             pltpu.SemaphoreType.DMA((5, 3)),
             pltpu.SemaphoreType.DMA((5, 3, 3)),
             pltpu.SemaphoreType.DMA((5, 3, 3)),
-            pltpu.SemaphoreType.DMA((3,)),
+            pltpu.SemaphoreType.DMA((6,)),
+            pltpu.SemaphoreType.DMA((8,)),
         ],
         compiler_params=pltpu.CompilerParams(
             collective_id=0, has_side_effects=True, vmem_limit_bytes=56 * 2**20
         ),
         name="layer",
-    )(coef, cot, w0, w1, w2, src, tgt, rot, gate, live)
+    )(coef, cot, w0, w1, w2, rot, src, tgt, gate, live)
 
 
 def shards(coeffs, cotangent, w_zero, w_one, w_two, source, target, rotation, gate, tile_live):
@@ -494,9 +547,9 @@
 
     upd, gco, grads = work(
         by_coef(coeffs), by_coef(cotangent), w_zero, w_one, w_two,
-        source, target, rotation[0], gate, tile_live,
+        rotation[0], source, target, gate, tile_live,
     )
-    whole = pl.BlockSpec(memory_space=pltpu.VMEM)
+    far = pl.BlockSpec(memory_space=pltpu.HBM)
     upd, gco, zero, one, two = pl.pallas_call(
         finish,
         out_shape=(
@@ -506,11 +559,18 @@
             jax.ShapeDtypeStruct((2, 512, 512), F32),
             jax.ShapeDtypeStruct((2, 256, 256), F32),
         ),
-        in_specs=[whole] * 3,
-        out_specs=(whole,) * 5,
-        compiler_params=pltpu.CompilerParams(vmem_limit_bytes=24 * 2**20),
+        in_specs=[far] * 3,
+        out_specs=(far,) * 5,
+        scratch_shapes=[
+            vmem(2, HALF, 128),
+            pltpu.VMEM((768, 768), F32),
+            pltpu.VMEM((2, 512, 512), F32),
+            pltpu.VMEM((2, 256, 256), F32),
+            pltpu.SemaphoreType.DMA((3 * len(RUNS) + 2,)),
+        ],
+        compiler_params=pltpu.CompilerParams(vmem_limit_bytes=62 * 2**20),
         name="finish",
-    )(upd, gco, grads)
+    )(upd, gco, grads.reshape(2, HALF, 128))
     return by_atom(upd), by_atom(gco), zero, one, two
 
 

time: 76.4 us -> 85.5 us (1.12)
  Pallas kernels: 71.9 us -> 84.5 us
  local copies, waits for them, and re-layouts: 3.62 us -> 0 us
    pallas_call x1, Pallas kernels: 2.84 us -> 19.2 us  [shards(): pl.pallas_call(finish, out_shape=(jax.ShapeDtypeStruct((NC * A, C), BF16)...]
    pallas_call x1, Pallas kernels: 69 us -> 65.4 us  [work(): pl.pallas_call(body, out_shape=(jax.ShapeDtypeStruct((NC * A, C), BF16),...]
    unnamed x6 -> x0, local copies, waits for them, and re-layouts: 3.62 us -> none
where the time goes in v2:
time: 85.5 us; the launch traced here: 85.3 us
  Pallas kernels  84.5 us (99%)
    pallas_call x1, Pallas kernels, work(): pl.pallas_call(body, out_shape=(jax.ShapeDtypeStruct((NC * A, C), BF16),...  65.4 us
    pallas_call x1, Pallas kernels, shards(): pl.pallas_call(finish, out_shape=(jax.ShapeDtypeStruct((NC * A, C), BF16)...  19.2 us

profile of v2, /device:TPU:1, one launch (start us, length us, event | category | flops | bytes accessed | tf_op | source)
XLA Modules:
  0.0 85.3 jit_solution(14137117840923531810)
XLA Ops:
  0.6 65.4 %layer.1 = (bf16[576,256]{1,0:T(8,128)(2,1)}, bf16[576,256]{1,0:T(8,128)(2,1)}, bf16[9728,128]{1,0:T(8,128)(2,1)}) custom-call(bf16[576,256]{1,0:T(8,128)(2,1)} %bitcast.23, bf16[576,256]{1,0:T(8,128)(2,1)} %bitcast.24, bf16[768,768]{1,0:T(8,128)(2,1)} %w0_in.1, bf16[2,512,512]{2,1,0:T(8,128)(2,1)} %w1_in.1, bf16[2,256,256]{2,1,0:T(8,128)(2,1)} %w2_in.1, ...), custom_call_target="tpu_custom_call" | custom-call | tf_op jit(solution)/shard_map/layer/pallas_call | solution.py:480
  66.0 19.2 %finish.1 = (bf16[576,256]{1,0:T(8,128)(2,1)}, bf16[576,256]{1,0:T(8,128)(2,1)}, f32[768,768]{1,0:T(8,128)}, f32[2,512,512]{2,1,0:T(8,128)}, f32[2,256,256]{2,1,0:T(8,128)}) custom-call(bf16[576,256]{1,0:T(8,128)(2,1)} %get-tuple-element.13.upd, bf16[576,256]{1,0:T(8,128)(2,1)} %get-tuple-element.14.gco, bf16[2,4864,128]{2,1,0:T(8,128)(2,1)} %bitcast.22), custom_call_target="tpu_custom_call" | custom-call | tf_op jit(solution)/shard_map/finish/pallas_call | solution.py:553

commit v3 on v2

--- a/solution.py
+++ b/solution.py
@@ -433,17 +433,20 @@
 RUNS = ((0, 3, 0, 0), (3, 3, 0, 1), (6, 4, 1, 0), (10, 3, 0, 2), (13, 4, 1, 1), (17, 2, 2, 0))
 
 
-def finish(upd, gco, O, upd_out, gco_out, g_zero, g_one, g_two, near, zero, one, two, sem):
+def finish(upd, gco, O, upd_out, gco_out, g_zero, g_one, g_two, near, rows_near, zero, one, two, sem):
     count = len(RUNS)
-    straight = [
-        pltpu.make_async_copy(upd, upd_out, sem.at[3 * count]),
-        pltpu.make_async_copy(gco, gco_out, sem.at[3 * count + 1]),
+    through = [
+        [
+            pltpu.make_async_copy(start, rows_near.at[i], sem.at[3 * count + 2 * i]),
+            pltpu.make_async_copy(rows_near.at[i], end, sem.at[3 * count + 2 * i + 1]),
+        ]
+        for i, (start, end) in enumerate(((upd, upd_out), (gco, gco_out)))
     ]
     reads = []
     for i, (t, n, _, _) in enumerate(RUNS):
         rows = pl.ds(t * C, n * C)
         reads.append(pltpu.make_async_copy(O.at[:, rows], near.at[:, rows], sem.at[i]))
-    for copy in reads + straight:
+    for copy in reads + [inward for inward, _ in through]:
         copy.start()
     writes = []
     for i, (t, n, kind, row) in enumerate(RUNS):
@@ -466,7 +469,11 @@
             )
             write.start()
             writes.append(write)
-    for copy in straight + writes:
+    for inward, outward in through:
+        inward.wait()
+        outward.start()
+        writes.append(outward)
+    for copy in writes:
         copy.wait()
 
 
@@ -563,10 +570,11 @@
         out_specs=(far,) * 5,
         scratch_shapes=[
             vmem(2, HALF, 128),
+            vmem(2, NC * A, C),
             pltpu.VMEM((768, 768), F32),
             pltpu.VMEM((2, 512, 512), F32),
             pltpu.VMEM((2, 256, 256), F32),
-            pltpu.SemaphoreType.DMA((3 * len(RUNS) + 2,)),
+            pltpu.SemaphoreType.DMA((3 * len(RUNS) + 4,)),
         ],
         compiler_params=pltpu.CompilerParams(vmem_limit_bytes=62 * 2**20),
         name="finish",

time: 85.5 us -> 70 us (0.82)
  Pallas kernels: 84.5 us -> 69 us
    pallas_call x1, Pallas kernels: 19.2 us -> 3.67 us  [shards(): pl.pallas_call(finish, out_shape=(jax.ShapeDtypeStruct((NC * A, C), BF16)...]
where the time goes in v3:
time: 70 us; the launch traced here: 69.8 us
  Pallas kernels  69 us (99%)
  between operations  0.8 us (1%)
    pallas_call x1, Pallas kernels, work(): pl.pallas_call(body, out_shape=(jax.ShapeDtypeStruct((NC * A, C), BF16),...  65.4 us
    pallas_call x1, Pallas kernels, shards(): pl.pallas_call(finish, out_shape=(jax.ShapeDtypeStruct((NC * A, C), BF16)...  3.67 us

profile of v3, /device:TPU:1, one launch (start us, length us, event | category | flops | bytes accessed | tf_op | source)
XLA Modules:
  0.0 69.8 jit_solution(1397848204011805406)
XLA Ops:
  0.6 65.4 %layer.1 = (bf16[576,256]{1,0:T(8,128)(2,1)}, bf16[576,256]{1,0:T(8,128)(2,1)}, bf16[9728,128]{1,0:T(8,128)(2,1)}) custom-call(bf16[576,256]{1,0:T(8,128)(2,1)} %bitcast.23, bf16[576,256]{1,0:T(8,128)(2,1)} %bitcast.24, bf16[768,768]{1,0:T(8,128)(2,1)} %w0_in.1, bf16[2,512,512]{2,1,0:T(8,128)(2,1)} %w1_in.1, bf16[2,256,256]{2,1,0:T(8,128)(2,1)} %w2_in.1, ...), custom_call_target="tpu_custom_call" | custom-call | tf_op jit(solution)/shard_map/layer/pallas_call | solution.py:487
  66.0 3.7 %finish.1 = (bf16[576,256]{1,0:T(8,128)(2,1)}, bf16[576,256]{1,0:T(8,128)(2,1)}, f32[768,768]{1,0:T(8,128)}, f32[2,512,512]{2,1,0:T(8,128)}, f32[2,256,256]{2,1,0:T(8,128)}) custom-call(bf16[576,256]{1,0:T(8,128)(2,1)} %get-tuple-element.13.upd, bf16[576,256]{1,0:T(8,128)(2,1)} %get-tuple-element.14.gco, bf16[2,4864,128]{2,1,0:T(8,128)(2,1)} %bitcast.22), custom_call_target="tpu_custom_call" | custom-call | tf_op jit(solution)/shard_map/finish/pallas_call | solution.py:560

commit v4 on v3

--- a/solution.py
+++ b/solution.py
@@ -281,7 +281,76 @@
     one = eye(C)
     for c in range(NC):
         cotT[pl.ds(c * C, C), :] = nt(one, cot[pl.ds(c * A, A), :]).astype(BF16)
-    for copy in loads[2:]:
+    loads[2].wait()
+
+    def gather(table, onehot, out, degrees):
+        def step(b, carry):
+            lane0 = pl.multiple_of(b * EB, EB)
+            pick = onehot[:, pl.ds(lane0, EB)]
+            for g in degrees:
+                for c in range(g * g, (g + 1) * (g + 1)):
+                    X[pl.ds(c * C, C), :] = nn(table[pl.ds(c * C, C), :], pick)
+                rotate(wide, X, NATURAL, out, POS, lane0, False, (g,))
+            return carry
+
+        lax.fori_loop(0, NB, step, 0)
+
+    def mix(zero, first, second, data, out, b):
+        lane0 = pl.multiple_of(b * EB, EB)
+        lanes = pl.ds(lane0, EB)
+        for m, r0, n in ((zero, 0, 768), (first, 768, 1024), (second, 1792, 512)):
+            right = data[pl.ds(r0, n), lanes]
+            for i in range(n // C):
+                X[pl.ds(r0 + i * C, C), :] = nn(m[pl.ds(i * C, C), :], right)
+        rotate(wide, X, POS, out, NATURAL, lane0, True)
+
+    def backward(lo, hi):
+        lax.fori_loop(lo, hi, lambda b, t: (mix(w0, M1b, M2b, hT, bT, b), t)[1], 0)
+
+    def forward(lo, hi):
+        lax.fori_loop(lo, hi, lambda b, t: (mix(W0T, M1f, M2f, yT, yT, b), t)[1], 0)
+
+    gather(cotT, oh_t, hT, (0, 1, 2))
+
+    def table(i, coefs):
+        for copy in halo[i]:
+            copy.wait_recv()
+        for c in coefs:
+            rows = pl.ds(c * A, A)
+            both = jnp.concatenate([T3[0, rows, :], coef[rows, :], T3[1, rows, :]], axis=0)
+            CT[pl.ds(c * C, C), :] = nt(one, both).astype(BF16)
+
+    def put(tile, value):
+        for k in range(2):
+            G[pl.ds(k * HALF + tile * C, C), :] = value[:, k * 128 : (k + 1) * 128].astype(BF16)
+
+    def zero_tiles(tile, i):
+        for j in range(3):
+            put(tile + j, nt(yT[pl.ds(i * C, C), :], hT[pl.ds(j * C, C), :]))
+
+    def pair_tiles(tile, a0, b0, n, i):
+        ya, yb = yT[pl.ds(a0 + i * C, C), :], yT[pl.ds(b0 + i * C, C), :]
+        for j in range(n):
+            ha, hb = hT[pl.ds(a0 + j * C, C), :], hT[pl.ds(b0 + j * C, C), :]
+            put(tile + j, nt(ya, ha) + nt(yb, hb))
+            put(tile + n + j, nt(ya, hb) - nt(yb, ha))
+
+    table(0, range(4))
+    gather(CT, oh_s, yT, (0, 1))
+    zero_tiles(0, 0)
+    zero_tiles(3, 1)
+    swap[0].start()
+    pair_tiles(6, 768, 1280, 2, 0)
+    table(1, range(4, 9))
+    advance(0, 0)
+    gather(CT, oh_s, yT, (2,))
+    zero_tiles(10, 2)
+    swap[1].start()
+    pair_tiles(13, 768, 1280, 2, 1)
+    pair_tiles(17, 1792, 2048, 1, 0)
+    swap[2].start()
+    advance(0, 1)
+    for copy in loads[3:]:
         copy.wait()
     for i in range(3):
         W0T[pl.ds(i * C, C), :] = nt(one, w0[:, pl.ds(i * C, C)]).astype(BF16)
@@ -299,79 +368,10 @@
             fwd[rows, hi] = (-imag).astype(BF16)
             fwd[next_rows, lo] = imag.astype(BF16)
             fwd[next_rows, hi] = real.astype(BF16)
-
-    def gather(table, onehot, out, degrees):
-        def step(b, carry):
-            lane0 = pl.multiple_of(b * EB, EB)
-            pick = onehot[:, pl.ds(lane0, EB)]
-            for g in degrees:
-                for c in range(g * g, (g + 1) * (g + 1)):
-                    X[pl.ds(c * C, C), :] = nn(table[pl.ds(c * C, C), :], pick)
-                rotate(wide, X, NATURAL, out, POS, lane0, False, (g,))
-            return carry
-
-        lax.fori_loop(0, NB, step, 0)
-
-    def mix(zero, first, second, data, out, b):
-        lane0 = pl.multiple_of(b * EB, EB)
-        lanes = pl.ds(lane0, EB)
-        for m, r0, n in ((zero, 0, 768), (first, 768, 1024), (second, 1792, 512)):
-            right = data[pl.ds(r0, n), lanes]
-            for i in range(n // C):
-                X[pl.ds(r0 + i * C, C), :] = nn(m[pl.ds(i * C, C), :], right)
-        rotate(wide, X, POS, out, NATURAL, lane0, True)
-
-    def backward(lo, hi):
-        lax.fori_loop(lo, hi, lambda b, t: (mix(w0, M1b, M2b, hT, bT, b), t)[1], 0)
-
-    def forward(lo, hi):
-        lax.fori_loop(lo, hi, lambda b, t: (mix(W0T, M1f, M2f, yT, yT, b), t)[1], 0)
-
-    gather(cotT, oh_t, hT, (0, 1, 2))
     backward(0, 1)
-
-    def table(i, coefs):
-        for copy in halo[i]:
-            copy.wait_recv()
-        for c in coefs:
-            rows = pl.ds(c * A, A)
-            both = jnp.concatenate([T3[0, rows, :], coef[rows, :], T3[1, rows, :]], axis=0)
-            CT[pl.ds(c * C, C), :] = nt(one, both).astype(BF16)
-
-    def put(tile, value):
-        for k in range(2):
-            G[pl.ds(k * HALF + tile * C, C), :] = value[:, k * 128 : (k + 1) * 128].astype(BF16)
-
-    def zero_tiles(tile, i):
-        for j in range(3):
-            put(tile + j, nt(yT[pl.ds(i * C, C), :], hT[pl.ds(j * C, C), :]))
-
-    def pair_tiles(tile, a0, b0, n, i):
-        ya, yb = yT[pl.ds(a0 + i * C, C), :], yT[pl.ds(b0 + i * C, C), :]
-        for j in range(n):
-            ha, hb = hT[pl.ds(a0 + j * C, C), :], hT[pl.ds(b0 + j * C, C), :]
-            put(tile + j, nt(ya, ha) + nt(yb, hb))
-            put(tile + n + j, nt(ya, hb) - nt(yb, ha))
-
-    table(0, range(4))
-    gather(CT, oh_s, yT, (0, 1))
-    zero_tiles(0, 0)
-    zero_tiles(3, 1)
-    swap[0].start()
-    pair_tiles(6, 768, 1280, 2, 0)
-    table(1, range(4, 9))
-    gather(CT, oh_s, yT, (2,))
-    advance(0, 0)
-    zero_tiles(10, 2)
-    swap[1].start()
-    pair_tiles(13, 768, 1280, 2, 1)
-    pair_tiles(17, 1792, 2048, 1, 0)
-    swap[2].start()
-    advance(0, 1)
-    backward(1, 2)
     advance(0, 2)
     advance(1, 0)
-    backward(2, 4)
+    backward(1, 4)
     advance(1, 1)
 
     def sum_back(coefs):
@@ -410,6 +410,7 @@
         upd[rows, :] = (coef[rows, :].astype(F32) + total).astype(BF16)
     stores[6].start()
     advance(4, 2)
+    advance(5, 0)
     for pair in give:
         for copy in pair:
             copy.wait_recv()
@@ -417,8 +418,8 @@
         (cot[...].astype(F32) + own_sum[...]) + (RB[0].astype(F32) + RB[1].astype(F32))
     ).astype(BF16)
     stores[7].start()
-    for p in range(3):
-        advance(5, p)
+    advance(5, 1)
+    advance(5, 2)
     for p in range(3):
         for copy in share[p]:
             copy.wait_recv()

time: 70 us -> 69.2 us (0.989)
  Pallas kernels: 69 us -> 68.2 us
    pallas_call x1, Pallas kernels: 65.4 us -> 64.5 us  [work(): pl.pallas_call(body, out_shape=(jax.ShapeDtypeStruct((NC * A, C), BF16),...]
where the time goes in v4:
time: 69.2 us; the launch traced here: 69 us
  Pallas kernels  68.2 us (99%)
  between operations  0.8 us (1%)
    pallas_call x1, Pallas kernels, work(): pl.pallas_call(body, out_shape=(jax.ShapeDtypeStruct((NC * A, C), BF16),...  64.5 us
    pallas_call x1, Pallas kernels, shards(): pl.pallas_call(finish, out_shape=(jax.ShapeDtypeStruct((NC * A, C), BF16)...  3.67 us

profile of v4, /device:TPU:1, one launch (start us, length us, event | category | flops | bytes accessed | tf_op | source)
XLA Modules:
  0.0 69.0 jit_solution(10375093153752934194)
XLA Ops:
  0.6 64.5 %layer.1 = (bf16[576,256]{1,0:T(8,128)(2,1)}, bf16[576,256]{1,0:T(8,128)(2,1)}, bf16[9728,128]{1,0:T(8,128)(2,1)}) custom-call(bf16[576,256]{1,0:T(8,128)(2,1)} %bitcast.23, bf16[576,256]{1,0:T(8,128)(2,1)} %bitcast.24, bf16[768,768]{1,0:T(8,128)(2,1)} %w0_in.1, bf16[2,512,512]{2,1,0:T(8,128)(2,1)} %w1_in.1, bf16[2,256,256]{2,1,0:T(8,128)(2,1)} %w2_in.1, ...), custom_call_target="tpu_custom_call" | custom-call | tf_op jit(solution)/shard_map/layer/pallas_call | solution.py:488
  65.1 3.7 %finish.1 = (bf16[576,256]{1,0:T(8,128)(2,1)}, bf16[576,256]{1,0:T(8,128)(2,1)}, f32[768,768]{1,0:T(8,128)}, f32[2,512,512]{2,1,0:T(8,128)}, f32[2,256,256]{2,1,0:T(8,128)}) custom-call(bf16[576,256]{1,0:T(8,128)(2,1)} %get-tuple-element.13.upd, bf16[576,256]{1,0:T(8,128)(2,1)} %get-tuple-element.14.gco, bf16[2,4864,128]{2,1,0:T(8,128)(2,1)} %bitcast.22), custom_call_target="tpu_custom_call" | custom-call | tf_op jit(solution)/shard_map/finish/pallas_call | solution.py:561
